TPU v7x, 32 devices: a whole 2x2x4 slice. The times are simulated.
32 devices in a mesh: groups: 2 (over y), gx: 4 (over z), gy: 4 (over x, core).
Axes of the slice: x: 2, y: 2, z: 4, core: 2. Of those that a mesh axis runs over, the one named last changes fastest.
Arguments:
- states: bfloat16 [48, 2, 8192], P('groups', None, 'gx'), parts along dimension 0, may hold values from -24 to 24
- lengths: int32 [48], P(('groups', 'gx')), parts along dimension 0, may hold values from 1 to 128, 1536 in all
- attn_gain: float32 [8192], P('gx'), may hold values from 0.25 to 1.75
- mlp_gain: float32 [8192], P('gx'), may hold values from 0.25 to 1.75
- w_qkv: bfloat16 [8192, 8, 1280], P('gx', 'gy'), may hold values from -0.0625 to 0.0625
- b_qkv: bfloat16 [8, 1280], P('gy'), may hold values from -3 to 3
- key_cache: bfloat16 [48, 128, 8, 128], P(('groups', 'gx'), None, 'gy'), parts along dimension 0, may hold values from -256 to 256
- value_cache: bfloat16 [48, 128, 8, 128], P(('groups', 'gx'), None, 'gy'), parts along dimension 0, may hold values from -6 to 6
- w_out: bfloat16 [8, 1024, 8192], P('gy', None, 'gx'), may hold values from -0.0625 to 0.0625
- w_gate_up: bfloat16 [8192, 2, 15360], P('gx', None, 'gy'), may hold values from -0.0625 to 0.0625
- w_down: bfloat16 [15360, 8192], P('gy', 'gx'), may hold values from -0.046875 to 0.046875
Outputs:
- layer_out: float32 [48, 2, 8192], P('groups', None, 'gx'), parts along dimension 0
There are 2 independent parts, one for each index of `groups`. A program takes and returns all parts, laid end to end along the dimension named above; an argument that names none is the same for every part. Nothing has to cross between parts.
Inputs may be any that keep to these rules, and one draw needn't show every extreme that they name: `lengths`: some rollout has exactly 128 cached tokens.
All inputs are finite; a program needn't handle non-finite values. No bound on the sum of `lengths` on one device may be relied on, other than what follows from the above.
Results may differ from a plain program's by a relative error of at most 0.017.
Values may be sent and summed in bfloat16 or wider, within the bound.
A program may use at most 192 MiB of HBM per device.

v0:
```python
import math

import jax
import jax.numpy as jnp
from jax import lax
from jax.sharding import PartitionSpec as P

norm_eps = 1e-06
rope_base = 1000000.0


def rotate(values, position):
    half = values.shape[-1] // 2
    inverse = rope_base ** (-(jnp.arange(half, dtype=jnp.float32) * 2.0 / values.shape[-1]))
    angle = position[..., None] * inverse
    cosine = jnp.cos(angle)
    sine = jnp.sin(angle)
    first = values[..., :half]
    second = values[..., half:]
    return jnp.concatenate(
        [first * cosine - second * sine, second * cosine + first * sine], axis=-1
    )


def attend(query, keys, values, key_cache, value_cache, lengths):
    slots_count = key_cache.shape[1]
    new_count = query.shape[1]
    scale = 1.0 / math.sqrt(query.shape[-1])
    old_scores = (
        jnp.einsum("rtkgh,rckh->rkgtc", query, key_cache, preferred_element_type=jnp.float32)
        * scale
    )
    new_scores = (
        jnp.einsum("rtkgh,rskh->rkgts", query, keys, preferred_element_type=jnp.float32) * scale
    )
    slots = jnp.arange(slots_count, dtype=jnp.int32)
    valid_old = (slots[None, :] < lengths[:, None])[:, None, None, None, :]
    order = jnp.arange(new_count, dtype=jnp.int32)
    valid_new = order[:, None] >= order[None, :]
    scores = jnp.concatenate(
        [jnp.where(valid_old, old_scores, -1e30), jnp.where(valid_new, new_scores, -1e30)], axis=-1
    )
    highest = jnp.max(scores, axis=-1, keepdims=True)
    raised = jnp.exp(scores - highest)
    weights = (raised / jnp.sum(raised, axis=-1, keepdims=True)).astype(jnp.bfloat16)
    from_cache = jnp.einsum(
        "rkgtc,rckh->rtkgh",
        weights[..., :slots_count],
        value_cache,
        preferred_element_type=jnp.float32,
    )
    from_new = jnp.einsum(
        "rkgts,rskh->rtkgh", weights[..., slots_count:], values, preferred_element_type=jnp.float32
    )
    return (from_cache + from_new).astype(jnp.bfloat16)


def on_device(
    states,
    lengths,
    attn_gain,
    mlp_gain,
    w_qkv,
    b_qkv,
    key_cache,
    value_cache,
    w_out,
    w_gate_up,
    w_down,
):
    rollouts, new_count, width_local = states.shape
    rows = rollouts * new_count
    model_width = width_local * lax.axis_size("gx")
    rows_local = rows // lax.axis_size("gx")
    owned = rows_local // new_count
    head_size = key_cache.shape[3]
    kv_local = w_qkv.shape[1]
    group = w_qkv.shape[2] // head_size - 2
    resid = states.astype(jnp.float32).reshape(rows, width_local)
    squares = lax.psum(jnp.sum(resid * resid, axis=1), "gx")
    normed = (resid * lax.rsqrt(squares / model_width + norm_eps)[:, None] * attn_gain).astype(
        jnp.bfloat16
    )
    flat_qkv = w_qkv.reshape(width_local, kv_local * (group + 2) * head_size)
    qkv = lax.psum_scatter(
        jnp.dot(normed, flat_qkv, preferred_element_type=jnp.float32).astype(jnp.bfloat16),
        "gx",
        scatter_dimension=0,
        tiled=True,
    ).astype(jnp.float32)
    qkv = qkv.reshape(owned, new_count, kv_local, group + 2, head_size) + b_qkv.astype(
        jnp.float32
    ).reshape(kv_local, group + 2, head_size)
    position = (lengths[:, None] + jnp.arange(new_count, dtype=jnp.int32)[None, :]).astype(
        jnp.float32
    )
    query = rotate(qkv[:, :, :, :group, :], position[:, :, None, None]).astype(jnp.bfloat16)
    keys = rotate(qkv[:, :, :, group, :], position[:, :, None]).astype(jnp.bfloat16)
    values = qkv[:, :, :, group + 1, :].astype(jnp.bfloat16)
    heads = attend(query, keys, values, key_cache, value_cache, lengths).reshape(
        rows_local, kv_local * group * head_size
    )
    flat_out = w_out.reshape(kv_local * group * head_size, width_local)
    attn_part = jnp.dot(
        lax.all_gather(heads, "gx", axis=0, tiled=True),
        flat_out,
        preferred_element_type=jnp.float32,
    )
    mixed = resid + lax.psum(attn_part.astype(jnp.bfloat16), "gy").astype(jnp.float32)
    squares_two = lax.psum(jnp.sum(mixed * mixed, axis=1), "gx")
    normed_two = (
        mixed * lax.rsqrt(squares_two / model_width + norm_eps)[:, None] * mlp_gain
    ).astype(jnp.bfloat16)
    hidden_local = w_gate_up.shape[2]
    flat_gate_up = w_gate_up.reshape(width_local, 2 * hidden_local)
    gate_up = (
        lax.psum_scatter(
            jnp.dot(normed_two, flat_gate_up, preferred_element_type=jnp.float32).astype(
                jnp.bfloat16
            ),
            "gx",
            scatter_dimension=0,
            tiled=True,
        )
        .astype(jnp.float32)
        .reshape(rows_local, 2, hidden_local)
    )
    hidden_share = (jax.nn.silu(gate_up[:, 0]) * gate_up[:, 1]).astype(jnp.bfloat16)
    down_part = jnp.dot(
        lax.all_gather(hidden_share, "gx", axis=0, tiled=True),
        w_down,
        preferred_element_type=jnp.float32,
    )
    layer_out = mixed + lax.psum(down_part.astype(jnp.bfloat16), "gy").astype(jnp.float32)
    return layer_out.reshape(rollouts, new_count, width_local)


def solution(mesh):
    in_specs = (
        P("groups", None, "gx"),
        P(("groups", "gx")),
        P("gx"),
        P("gx"),
        P("gx", "gy", None),
        P("gy", None),
        P(("groups", "gx"), None, "gy", None),
        P(("groups", "gx"), None, "gy", None),
        P("gy", None, "gx"),
        P("gx", None, "gy"),
        P("gy", "gx"),
    )
    out_specs = P("groups", None, "gx")
    return jax.shard_map(
        on_device, mesh=mesh, in_specs=in_specs, out_specs=out_specs, check_vma=False
    )
```

profile of v0, /device:TPU:1, one launch (start us, length us, event | category | flops | bytes accessed | tf_op | source)
XLA Modules:
  0.0 230.4 jit_solution(7342147593973681726)
XLA Ops:
  6.5 0.0 copy-start
  6.5 0.0 all-reduce.7.cloned.1.call-start
  6.5 1.3 multiply_reduce_fusion.1
  7.8 0.1 reduce_sum.30
  7.9 10.8 %psum.28 = f32[48]{0:T(128)S(1)} all-reduce(f32[48]{0:T(128)S(1)} %reduce_sum.30), channel_id=1, replica_groups=mesh['groups'=2,'gx'=4,'gy'=4] {'gx'}, use_global_device_ids=true, to_apply=%region_1.0 | all-reduce | flops 48 | bytes 384 | tf_op jit(solution)/shard_map/psum | solution.py:80
  18.7 0.1 mul.163
  18.8 1.2 multiply_convert_fusion.1
  20.0 0.1 convert_element_type.61
  20.1 10.2 %copy.51 = bf16[256,8,2,1280]{3,1,2,0:T(8,128)(2,1)} copy(bf16[256,8,2,1280]{3,2,1,0:T(2,128)(2,1)} %bitcast.83) | data formatting | bytes 20971520
  30.3 5.9 %convolution_convert_fusion.1 = bf16[48,2560]{1,0:T(8,128)(2,1)S(1)} fusion(bf16[48,2048]{1,0:T(8,128)(2,1)S(1)} %convert_element_type.61, bf16[2048,2560]{1,0:T(8,128)(2,1)} %bitcast.80), kind=kOutput, calls=%fused_computation.1 | convolution fusion | flops 503439360 | bytes 10928128 | tf_op jit(solution)/shard_map/dot_general | solution.py:86
  36.2 11.1 %fusion = bf16[16,2560]{1,0:T(8,128)(2,1)S(1)} fusion(bf16[48,2560]{1,0:T(8,128)(2,1)S(1)} %convolution_convert_fusion.1), kind=kCustom, calls=%all-reduce-scatter | all-reduce-scatter fusion | flops 163841 | bytes 328192
  47.3 1.5 collective-permute-start
  48.9 0.0 copy-done.7
  48.9 0.1 iota_compare_fusion
  49.0 0.1 add_convert_fusion.2
  49.1 0.0 copy-done.6
  49.1 0.0 copy-done.8
  49.1 0.6 dynamic-slice.6
  50.3 0.2 multiply_cosine_fusion
  50.5 0.0 collective-permute-done
  50.5 0.2 concatenate.14
  50.8 0.0 copy-start.3
  50.9 0.1 subtract_convert_fusion
  51.0 0.1 subtract_convert_fusion.1
  51.1 0.0 copy-done
  51.1 0.4 fusion.31
  51.6 0.3 fusion.32
  51.9 0.2 fusion.20
  52.1 0.1 divide_convert_fusion
  52.2 0.0 copy-done.4
  52.3 0.2 convolution_bitcast_fusion.1
  52.5 0.1 fusion.7
  52.6 0.1 reshape.158
  52.7 10.9 %all-gather = bf16[4,12,2048]{2,1,0:T(8,128)(2,1)S(1)} all-gather(bf16[1,12,2048]{2,1,0:T(8,128)(2,1)S(1)} %reshape.158), channel_id=1, replica_groups=mesh['groups'=2,'gx'=4,'gy'=4] {'gx'}, dimensions={0}, use_global_device_ids=true | all-gather | bytes 245760 | tf_op jit(solution)/shard_map/all_gather | solution.py:105
  63.6 5.6 %convolution_convert_fusion.3 = bf16[48,2048]{1,0:T(8,128)(2,1)} fusion(bf16[48,2048]{1,0:T(8,128)(2,1)S(1)} %reshape.159, bf16[2048,2048]{1,0:T(8,128)(2,1)} %bitcast.82), kind=kOutput, calls=%fused_computation.3 | convolution fusion | flops 402751488 | bytes 8781824 | tf_op jit(solution)/shard_map/dot_general | solution.py:104
  69.3 0.0 all-reduce.7.cloned.1.call-update
  69.3 0.0 all-reduce.9.cloned.1.call-start
  69.3 0.0 copy-done.3
  69.3 0.1 reshape.143
  69.4 0.0 copy-start.5
  69.4 21.8 %copy.52 = bf16[256,8,2,3840]{3,1,2,0:T(8,128)(2,1)} copy(bf16[256,8,2,3840]{3,2,1,0:T(2,128)(2,1)} %bitcast.81) | data formatting | bytes 62914560
  91.3 17.8 %all-reduce.7.cloned.1.call-done = bf16[48,2048]{1,0:T(8,128)(2,1)} async-done(((bf16[48,2048]{1,0:T(8,128)(2,1)}), bf16[48,2048]{1,0:T(8,128)(2,1)}) %all-reduce.7.cloned.1.call-update) | async-done | bytes 196624 | tf_op jit(solution)/shard_map/psum | solution.py:109
  109.0 1.1 multiply_reduce_fusion
  110.1 10.2 %psum.30 = f32[48]{0:T(128)S(1)} all-reduce(f32[48]{0:T(128)S(1)} %multiply_reduce_fusion), channel_id=1, replica_groups=mesh['groups'=2,'gx'=4,'gy'=4] {'gx'}, use_global_device_ids=true, to_apply=%region_8.9 | all-reduce | flops 48 | bytes 384 | tf_op jit(solution)/shard_map/psum | solution.py:110
  120.4 0.0 copy-done.5
  120.4 15.7 %convolution_convert_fusion = bf16[48,7680]{1,0:T(8,128)(2,1)S(1)} fusion(bf16[2048,7680]{1,0:T(8,128)(2,1)} %bitcast.79, f32[2048]{0:T(1024)S(1)} %copy-done.5, f32[48]{0:T(128)S(1)} %add_rsqrt_fusion, f32[48,2048]{1,0:T(8,128)S(1)} %reshape.143, bf16[48,2048]{1,0:T(8,128)(2,1)} %all-reduce.7.cloned.1.call-done), kind=kOutput, calls=%fused_computation | convolution fusion | flops 1510809600 | bytes 32792768 | tf_op jit(solution)/shard_map/dot_general | solution.py:118
  136.1 17.7 %fusion.1 = bf16[16,7680]{1,0:T(8,128)(2,1)S(1)} fusion(bf16[48,7680]{1,0:T(8,128)(2,1)S(1)} %convolution_convert_fusion), kind=kCustom, calls=%all-reduce-scatter.1 | all-reduce-scatter fusion | flops 491521 | bytes 983552
  153.7 0.1 slice.55
  153.8 1.3 collective-permute-start.1
  155.1 3.6 %collective-permute-done.1 = bf16[12,7680]{1,0:T(8,128)(2,1)S(1)} collective-permute-done((bf16[12,7680]{1,0:T(8,128)(2,1)S(1)}, bf16[12,7680]{1,0:T(8,128)(2,1)S(1)}, u32[]{:S(2)}, u32[]{:S(2)}) %collective-permute-start.1) | collective-permute-done | bytes 184352
  158.7 0.7 concatenate.15
  159.4 0.1 dynamic-slice_convert_fusion
  159.5 0.2 reshape.157
  159.7 0.3 fusion.30
  160.0 0.1 fusion.21
  160.1 12.8 %all-gather.1 = bf16[4,12,3840]{2,1,0:T(8,128)(2,1)S(1)} all-gather(bf16[1,12,3840]{2,1,0:T(8,128)(2,1)S(1)} %fusion.21), channel_id=1, replica_groups=mesh['groups'=2,'gx'=4,'gy'=4] {'gx'}, dimensions={0}, use_global_device_ids=true | all-gather | bytes 460800 | tf_op jit(solution)/shard_map/all_gather | solution.py:130
  172.9 0.1 reshape.161
  173.0 0.0 copy-start.2
  173.0 9.1 %convolution_convert_fusion.2 = bf16[48,2048]{1,0:T(8,128)(2,1)} fusion(bf16[48,3840]{1,0:T(8,128)(2,1)S(1)} %reshape.161, bf16[3840,2048]{1,0:T(8,128)(2,1)} %param.21), kind=kOutput, calls=%fused_computation.2 | convolution fusion | flops 755073024 | bytes 16293888 | tf_op jit(solution)/shard_map/dot_general | solution.py:129
  182.0 0.0 all-reduce.9.cloned.1.call-update
  182.1 39.5 %all-reduce.9.cloned.1.call-done = bf16[48,2048]{1,0:T(8,128)(2,1)} async-done(((bf16[48,2048]{1,0:T(8,128)(2,1)}), bf16[48,2048]{1,0:T(8,128)(2,1)}) %all-reduce.9.cloned.1.call-update) | async-done | bytes 196624 | tf_op jit(solution)/shard_map/psum | solution.py:134
  221.6 0.0 copy-done.2
  221.6 1.0 convert_add_fusion
  222.6 1.0 reshape.152
  (20 shorter events, 0.3 us)
Async XLA Ops:
  6.5 44.6 %copy-start = (bf16[6,128,2,128]{3,2,1,0:T(2,128)(2,1)S(1)}, bf16[6,128,2,128]{3,2,1,0:T(2,128)(2,1)}, u32[]{:S(2)}) copy-start(bf16[6,128,2,128]{3,2,1,0:T(2,128)(2,1)} %param.17) | copy-start | bytes 1179652
  6.5 102.5 %all-reduce.7.cloned.1.call-start = ((), (), s32[]{:S(2)}) async-start(), calls=%async_computation | async-start | bytes 393216 | tf_op jit(solution)/shard_map/psum | solution.py:109
  30.3 18.6 %copy-start.7 = (s32[6]{0:T(128)S(1)}, s32[6]{0:T(128)}, u32[]{:S(2)}) copy-start(s32[6]{0:T(128)} %param.12) | copy-start | bytes 76
  30.3 18.8 %copy-start.6 = (bf16[2,1280]{1,0:T(2,128)(2,1)S(1)}, bf16[2,1280]{1,0:T(2,128)(2,1)}, u32[]{:S(2)}) copy-start(bf16[2,1280]{1,0:T(2,128)(2,1)} %param.16) | copy-start | bytes 15364
  30.3 18.8 %copy-start.8 = (u32[32]{0:T(128)S(1)}, u32[32]{0:T(128)}, u32[]{:S(2)}) copy-start(u32[32]{0:T(128)} %constant.34) | copy-start | bytes 388
  30.3 21.9 %copy-start.4 = (bf16[6,128,2,128]{3,2,1,0:T(2,128)(2,1)S(1)}, bf16[6,128,2,128]{3,2,1,0:T(2,128)(2,1)}, u32[]{:S(2)}) copy-start(bf16[6,128,2,128]{3,2,1,0:T(2,128)(2,1)} %param.18) | copy-start | bytes 1179652
  47.3 3.2 %collective-permute-start = (bf16[12,2560]{1,0:T(8,128)(2,1)S(1)}, bf16[12,2560]{1,0:T(8,128)(2,1)S(1)}, u32[]{:S(2)}, u32[]{:S(2)}) collective-permute-start(bf16[12,2560]{1,0:T(8,128)(2,1)S(1)} %slice.54), channel_id=1, source_target_pairs={{0,4},{4,8},{8,12},{1,5},{5,9},{9,13},{2,6},{6,10},{10,14},{3,7},{... | collective-permute-start | bytes 184328
  50.8 18.6 %copy-start.3 = (bf16[24,2,2048]{2,1,0:T(2,128)(2,1)S(1)}, bf16[24,2,2048]{2,1,0:T(2,128)(2,1)}, u32[]{:S(2)}) copy-start(bf16[24,2,2048]{2,1,0:T(2,128)(2,1)} %param.11) | copy-start | bytes 589828
  69.3 152.3 %all-reduce.9.cloned.1.call-start = ((), (), s32[]{:S(2)}) async-start(), calls=%async_computation.1 | async-start | bytes 393216 | tf_op jit(solution)/shard_map/psum | solution.py:134
  69.4 51.0 %copy-start.5 = (f32[2048]{0:T(1024)S(1)}, f32[2048]{0:T(1024)}, u32[]{:S(2)}) copy-start(f32[2048]{0:T(1024)} %param.14) | copy-start | bytes 24580
  153.8 4.9 %collective-permute-start.1 = (bf16[12,7680]{1,0:T(8,128)(2,1)S(1)}, bf16[12,7680]{1,0:T(8,128)(2,1)S(1)}, u32[]{:S(2)}, u32[]{:S(2)}) collective-permute-start(bf16[12,7680]{1,0:T(8,128)(2,1)S(1)} %slice.55), channel_id=1, source_target_pairs={{0,4},{4,8},{8,12},{1,5},{5,9},{9,13},{2,6},{6,10},{10,14},{3,7},{... | collective-permute-start | bytes 552968
  172.9 50.6 %copy-start.1 = (bf16[6,128,2,128]{3,2,1,0:T(2,128)(2,1)S(1)}, bf16[6,128,2,128]{3,2,1,0:T(2,128)(2,1)}, u32[]{:S(2)}) copy-start(bf16[6,128,2,128]{3,2,1,0:T(2,128)(2,1)} %param.17) | copy-start | bytes 1179652
  173.0 48.6 %copy-start.2 = (bf16[48,2048]{1,0:T(8,128)(2,1)S(1)}, bf16[48,2048]{1,0:T(8,128)(2,1)}, u32[]{:S(2)}) copy-start(bf16[48,2048]{1,0:T(8,128)(2,1)} %all-reduce.7.cloned.1.call-done) | copy-start | bytes 589828
Sparse Core Ops, SparseCore 0:
  69.4 39.5 all-reduce.6
  182.2 39.3 all-reduce.8
where the time goes:
time: 233 us; the launch traced here: 230 us
  blocking collectives  73.5 us (32%)
  waiting for transfers between devices  60.9 us (26%)
  matrix products  37.3 us (16%)
  local copies, waits for them, and re-layouts  35.7 us (15%)
  between operations  14.4 us (6%)
  other arithmetic  5.61 us (2%)
  starting transfers between devices  2.88 us (1%)
    psum x1, waiting for transfers between devices, on_device(): lax.psum(down_part.astype(jnp.bfloat16), 'gy').astype(jnp.float32)  39.5 us
    unnamed x28, local copies, waits for them, and re-layouts  33.8 us
    unnamed x2, blocking collectives  28.8 us
    psum x1, waiting for transfers between devices, on_device(): lax.psum(attn_part.astype(jnp.bfloat16), 'gy').astype(jnp.float32)  17.8 us
    dot_general x1, matrix products, on_device(): jnp.dot(normed_two, flat_gate_up, preferred_element_type=jnp.float32)  15.7 us
    all_gather x1, blocking collectives, on_device(): lax.all_gather(hidden_share, 'gx', axis=0, tiled=True)  12.8 us
    all_gather x1, blocking collectives, on_device(): lax.all_gather(heads, 'gx', axis=0, tiled=True)  10.9 us
    psum x1, blocking collectives, on_device(): squares = lax.psum(jnp.sum(resid * resid, axis=1), 'gx')  10.8 us
  transfers between devices with their start and end apart: 4, of which 3 were waited for; matrix products, arithmetic and copies ran while one was open for 10% of the time, Pallas kernels for 0%

commit v1 on v0

v1 whole, which is shorter than its diff:
```python
import functools
import math

import jax
import jax.numpy as jnp
from jax import lax
from jax.experimental import pallas as pl
from jax.experimental.pallas import tpu as pltpu
from jax.sharding import PartitionSpec as P

norm_eps = 1e-06
rope_base = 1000000.0
LANES = 128
MESH = pl.DeviceIdType.MESH
bf16 = jnp.bfloat16
f32 = jnp.float32


def iota(shape, dim):
    return lax.broadcasted_iota(jnp.int32, shape, dim)


def each(count, body):
    if count <= 4:
        for i in range(count):
            body(i)
    else:

        def step(i, carry):
            body(i)
            return carry

        lax.fori_loop(0, count, step, 0)


class Sizes:
    def __init__(self, nx, ny, rows, width, kv, slots, hidden, group, new):
        self.nx, self.ny, self.width, self.kv, self.slots = nx, ny, width, kv, slots
        self.hidden, self.group, self.new = hidden, group, new
        self.rl = rows // nx
        self.rb = -(-self.rl // 16) * 16
        self.rp = nx * self.rb
        self.owned = self.rl // new
        self.qw = (group + 2) * LANES
        self.qcb = self.qw // LANES
        self.hcb = hidden // LANES
        self.pair = 2 if self.hcb % 2 == 0 else 1
        per = self.hcb // self.pair
        self.cb = max(c for c in range(1, 4) if per % c == 0)
        self.cw = self.cb * LANES
        self.msgs = per // self.cb
        self.mr = -(-(self.pair * 2 * self.rl) // 16) * 16
        self.dcb = width // LANES
        self.ra = self.rp // ny
        self.reuse = min(self.qcb, self.dcb) if width * kv >= hidden else 0
        fits = 2 * kv * group * LANES >= hidden
        self.second = self.reuse + (min(self.dcb - self.reuse, self.dcb // 2) if fits else 0)


def spread(pieces, target, sz):
    m = pieces[0].shape[0]
    total = None
    for h, piece in enumerate(pieces):
        stacked = jnp.concatenate(
            [piece[:, b * LANES : (b + 1) * LANES] for b in range(sz.dcb)], axis=0
        )
        place = (iota((LANES, 2 * LANES), 1) == 2 * iota((LANES, 2 * LANES), 0) + h).astype(bf16)
        d = jnp.dot(stacked, place, preferred_element_type=f32)
        total = d if total is None else total + d
    total = total.astype(bf16)
    for b in range(sz.dcb):
        target[:, b * 2 * LANES : (b + 1) * 2 * LANES] = total[b * m : (b + 1) * m]


def kernel(
    sz,
    model_width,
    lens,
    x_ref,
    ag_ref,
    mg_ref,
    bq_ref,
    wq_hbm,
    kc_hbm,
    vc_hbm,
    wo_hbm,
    wg_hbm,
    wd_hbm,
    out_ref,
    wq,
    wo,
    wg,
    wd,
    kc,
    vc,
    lhs,
    sq,
    rq,
    ss_s,
    ss_r,
    qb,
    nk,
    nv,
    heads,
    pa,
    pr,
    pall,
    mixed,
    ts_s,
    ts_r,
    sg,
    rg,
    hid,
    dr,
    dall,
    wq_sem,
    wo_sem,
    wg_sem,
    wd_sem,
    kv_sem,
    q_ss,
    q_rs,
    s_ss,
    s_rs,
    h_ss,
    h_rs,
    a_ss,
    a_rs,
    b_ss,
    b_rs,
    t_ss,
    t_rs,
    g_ss,
    g_rs,
    u_ss,
    u_rs,
    c_ss,
    c_rs,
    d_ss,
    d_rs,
):
    nx, ny, rb, rp, kv, rl = sz.nx, sz.ny, sz.rb, sz.rp, sz.kv, sz.rl
    mx, my = lax.axis_index("gx"), lax.axis_index("gy")
    lhs_q = lhs.at[pl.ds(0, kv * rp), pl.ds(0, kv * sz.width)]
    lhs_g = lhs.at[pl.ds(0, 2 * rl * nx)]

    def px(d):
        return lax.rem(mx + d, nx)

    def py(d):
        return lax.rem(my + d, ny)

    def lane(i, n):
        return pl.ds(pl.multiple_of(i * n, n), n)

    def wq_copy(i):
        if kv == 1:
            return pltpu.make_async_copy(wq_hbm.at[:, lane(i, LANES)], wq.at[i], wq_sem.at[i])
        return pltpu.make_async_copy(wq_hbm.at[:, :, lane(i, LANES)], wq.at[i], wq_sem.at[i])

    def wq_tile(i):
        if kv == 1:
            return wq.at[i]
        return wq.at[i].reshape(kv * sz.width, LANES)

    def wg_copy(i):
        return pltpu.make_async_copy(wg_hbm.at[:, :, lane(i, LANES)], wg.at[i], wg_sem.at[i])

    def wg_tile(i):
        return wg.at[i].reshape(2 * sz.width, LANES)

    hw = kv * sz.group * LANES

    def wo_copy(i, b):
        return pltpu.make_async_copy(
            wo_hbm.at[:, lane(2 * i + b, LANES)], wo.at[i, pl.ds(b * hw, hw)], wo_sem.at[i, b]
        )

    def wd_tile(i):
        if i < sz.reuse:
            return wq_tile(i).at[pl.ds(0, sz.hidden)]
        if i < sz.second:
            return wo.at[i - sz.reuse, pl.ds(0, sz.hidden)]
        return wd.at[i - sz.second]

    def wd_copy(i):
        return pltpu.make_async_copy(
            wd_hbm.at[:, pl.ds(i * LANES, LANES)], wd_tile(i), wd_sem.at[i]
        )

    kc_copy = pltpu.make_async_copy(kc_hbm, kc, kv_sem.at[0])
    vc_copy = pltpu.make_async_copy(vc_hbm, vc, kv_sem.at[1])
    each(sz.qcb, lambda i: wq_copy(i).start())
    kc_copy.start()
    vc_copy.start()
    for b in range(2):
        each(sz.dcb // 2, lambda i: wo_copy(i, b).start())
    each(sz.hcb, lambda i: wg_copy(i).start())
    for i in range(sz.second, sz.dcb):
        wd_copy(i).start()

    barrier = pltpu.get_barrier_semaphore()

    def greet(axis, who, n):
        each(
            n - 1,
            lambda d: pl.semaphore_signal(
                barrier, inc=1, device_id={axis: who(d + 1)}, device_id_type=MESH
            ),
        )

    greet("gx", px, nx)
    greet("gy", py, ny)

    def remote(src, dst, ss, rs, axis, peer):
        return pltpu.make_async_remote_copy(
            src_ref=src, dst_ref=dst, send_sem=ss, recv_sem=rs,
            device_id={axis: peer}, device_id_type=MESH,
        )

    resid = x_ref[...].astype(f32)
    square = jnp.sum(resid * resid, axis=1, keepdims=True)
    ss_s[...] = jnp.broadcast_to(square, (rp, LANES)).reshape(nx, rb, LANES)
    xg = (resid * ag_ref[...]).astype(bf16)
    if kv == 1:
        lhs_q[...] = xg
    else:
        zero = jnp.zeros_like(xg)
        spread(
            [jnp.concatenate([xg, zero], axis=0), jnp.concatenate([zero, xg], axis=0)], lhs_q, sz
        )
    pl.semaphore_wait(barrier, nx - 1 + ny - 1)

    def s_send(d):
        p = px(d + 1)
        return remote(ss_s.at[p], ss_r.at[mx], s_ss.at[p], s_rs.at[mx], "gx", p)

    each(nx - 1, lambda d: s_send(d).start())
    ss_r[mx] = ss_s[mx]

    def qkv_cols(i, carry):
        wq_copy(2 * i).wait()
        wq_copy(2 * i + 1).wait()
        right = jnp.concatenate([wq_tile(2 * i)[...], wq_tile(2 * i + 1)[...]], axis=1)
        part = jnp.dot(lhs_q[...], right, preferred_element_type=f32).astype(bf16)
        for h in range(kv):
            at = pl.multiple_of(h * sz.qw + i * 2 * LANES, 2 * LANES)
            sq[:, :, pl.ds(at, 2 * LANES)] = part[h * rp : (h + 1) * rp].reshape(nx, rb, 2 * LANES)
        return carry

    lax.fori_loop(0, sz.qcb // 2, qkv_cols, 0)

    def q_send(d):
        p = px(d + 1)
        return remote(sq.at[p], rq.at[mx], q_ss.at[p], q_rs.at[mx], "gx", p)

    each(nx - 1, lambda d: q_send(d).start())
    for i in range(sz.reuse):
        wd_copy(i).start()

    rq[mx] = sq[mx]

    def gathered(buf_s, buf_r, ss, rs, d):
        p = px(d + 1)
        return remote(buf_s.at[p], buf_r.at[p], ss.at[p], rs.at[p], "gx", p)

    row = iota((rb, LANES), 0)
    length_row = jnp.zeros((rb, LANES), jnp.int32)
    for r in range(sz.owned):
        length_row = jnp.where(row // sz.new == r, lens[r], length_row)
    position = (length_row + row % sz.new).astype(f32)
    half = LANES // 2
    lane_i = (iota((rb, LANES), 1) % half).astype(f32)
    angle = position * jnp.exp(lane_i * (-2.0 * math.log(rope_base) / LANES))
    cosine = jnp.cos(angle)
    sine = jnp.where(iota((rb, LANES), 1) < half, -jnp.sin(angle), jnp.sin(angle))

    each(nx - 1, lambda d: gathered(ss_s, ss_r, s_ss, s_rs, d).wait_recv())
    each(nx - 1, lambda d: gathered(sq, rq, q_ss, q_rs, d).wait_recv())

    def add_up(buf, n):
        if n <= 4:
            total = buf[0].astype(f32)
            for j in range(1, n):
                total = total + buf[j].astype(f32)
            return total
        return lax.fori_loop(
            1, n, lambda j, t: t + buf[j].astype(f32), buf[0].astype(f32)
        )

    scale = lax.rsqrt(add_up(ss_r, nx)[:, :1] / model_width + norm_eps)
    qkv = add_up(rq, nx) * scale + bq_ref[...].astype(f32)

    def rotate(v):
        return (v * cosine + pltpu.roll(v, half, 1) * sine).astype(bf16)

    nk[...] = jnp.zeros_like(nk)
    nv[...] = jnp.zeros_like(nv)
    for h in range(kv):
        base = h * sz.qw
        for g in range(sz.group):
            at = (h * sz.group + g) * rb
            qb[at : at + rb] = rotate(qkv[:, base + g * LANES : base + (g + 1) * LANES])
        at = base + sz.group * LANES
        nk[h * rb : (h + 1) * rb] = rotate(qkv[:, at : at + LANES])
        nv[h * rb : (h + 1) * rb] = qkv[:, at + LANES : at + 2 * LANES].astype(bf16)

    kc_copy.wait()
    vc_copy.wait()
    old = sz.owned * sz.slots * kv

    def flat(ref):
        return ref[...] if kv == 1 else ref.reshape(old, LANES)[...]

    trans = (((1,), (1,)), ((), ()))
    query = qb[...]
    qrows = kv * sz.group * rb
    s_old = lax.dot_general(query, flat(kc), trans, preferred_element_type=f32)
    s_new = lax.dot_general(query, nk[...], trans, preferred_element_type=f32)
    rid = iota((qrows, 1), 0)
    r_head, r_roll, r_tok = rid // (sz.group * rb), (rid % rb) // sz.new, rid % sz.new
    cid = iota((1, old), 1)
    c_roll = cid // (sz.slots * kv)
    limit = jnp.zeros((1, old), jnp.int32)
    for r in range(sz.owned):
        limit = jnp.where(c_roll == r, lens[r], limit)
    c_key = jnp.where((cid // kv) % sz.slots < limit, c_roll * kv + cid % kv, -1)
    r_key = r_roll * kv + r_head
    nid = iota((1, nk.shape[0]), 1)
    n_key = jnp.where(nid < kv * rb, ((nid % rb) // sz.new) * kv + nid // rb, -1)
    inv = 1.0 / math.sqrt(LANES)
    s_old = jnp.where(r_key == c_key, s_old * inv, -1e30)
    s_new = jnp.where((r_key == n_key) & (nid % sz.new <= r_tok), s_new * inv, -1e30)
    top = jnp.maximum(
        jnp.max(s_old, axis=1, keepdims=True), jnp.max(s_new, axis=1, keepdims=True)
    )
    e_old = jnp.exp(s_old - top)
    e_new = jnp.exp(s_new - top)
    norm = 1.0 / (jnp.sum(e_old, axis=1, keepdims=True) + jnp.sum(e_new, axis=1, keepdims=True))
    attn = jnp.dot((e_old * norm).astype(bf16), flat(vc), preferred_element_type=f32)
    attn = attn + jnp.dot((e_new * norm).astype(bf16), nv[...], preferred_element_type=f32)
    attn = attn.astype(bf16)
    for b in range(kv * sz.group):
        heads[mx, :, b * LANES : (b + 1) * LANES] = attn[b * rb : (b + 1) * rb]

    def h_send(d):
        p = px(d + 1)
        return remote(heads.at[mx], heads.at[mx], h_ss.at[p], h_rs.at[mx], "gx", p)

    def h_recv(d):
        p = px(d + 1)
        return remote(heads.at[p], heads.at[p], h_ss.at[p], h_rs.at[p], "gx", p)

    each(nx - 1, lambda d: h_send(d).start())
    each(nx - 1, lambda d: h_recv(d).wait_recv())

    def all_reduce(src, got, full, ss, rs, ss2, rs2):
        def send(d):
            p = py(d + 1)
            return remote(src.at[p], got.at[my], ss.at[p], rs.at[my], "gy", p)

        def recv(d):
            p = py(d + 1)
            return remote(src.at[p], got.at[p], ss.at[p], rs.at[p], "gy", p)

        each(ny - 1, lambda d: send(d).start())
        got[my] = src[my]
        each(ny - 1, lambda d: recv(d).wait_recv())
        full[my] = add_up(got, ny).astype(bf16)

        def send2(d):
            p = py(d + 1)
            return remote(full.at[my], full.at[my], ss2.at[p], rs2.at[my], "gy", p)

        def recv2(d):
            p = py(d + 1)
            return remote(full.at[p], full.at[p], ss2.at[p], rs2.at[p], "gy", p)

        each(ny - 1, lambda d: send2(d).start())
        each(ny - 1, lambda d: recv2(d).wait_recv())
        each(ny - 1, lambda d: send(d).wait_send())
        each(ny - 1, lambda d: send2(d).wait_send())
        return full[...].astype(f32).reshape(rp, sz.width)

    step = 2 * LANES

    def out_cols(i, carry):
        left = heads[...].reshape(rp, kv * sz.group * LANES)
        wo_copy(i, 0).wait()
        wo_copy(i, 1).wait()
        right = jnp.concatenate([wo[i, 0:hw], wo[i, hw : 2 * hw]], axis=1)
        part = jnp.dot(left, right, preferred_element_type=f32)
        pa[:, :, lane(i, step)] = part.astype(bf16).reshape(ny, sz.ra, step)
        return carry

    lax.fori_loop(0, sz.width // step, out_cols, 0)
    for i in range(sz.reuse, sz.second):
        wd_copy(i).start()
    mixed[...] = x_ref[...].astype(f32) + all_reduce(pa, pr, pall, a_ss, a_rs, b_ss, b_rs)

    m = mixed[...]
    square = jnp.sum(m * m, axis=1, keepdims=True)
    ts_s[...] = jnp.broadcast_to(square, (rp, LANES)).reshape(nx, rb, LANES)

    def t_send(d):
        p = px(d + 1)
        return remote(ts_s.at[p], ts_r.at[mx], t_ss.at[p], t_rs.at[mx], "gx", p)

    each(nx - 1, lambda d: t_send(d).start())
    ts_r[mx] = ts_s[mx]
    mg = (m * mg_ref[...]).astype(bf16)
    lr = 2 * rl * nx
    want = iota((lr, rp), 0)
    have = iota((lr, rp), 1)
    inside = want % (2 * rl)
    picks = []
    for h in range(2):
        source = (want // (2 * rl)) * rb + inside - h * rl
        chosen = (have == source) & (inside >= h * rl) & (inside < (h + 1) * rl)
        picks.append(
            jnp.dot(chosen.astype(bf16), mg, preferred_element_type=f32).astype(bf16)
        )
    spread(picks, lhs_g, sz)

    def gate_cols(i, carry):
        parts = []
        for a in range(sz.pair):
            for c in range(sz.cb):
                wg_copy((i * sz.pair + a) * sz.cb + c).wait()
        for a in range(sz.pair):
            first = (i * sz.pair + a) * sz.cb
            right = jnp.concatenate([wg_tile(first + c)[...] for c in range(sz.cb)], axis=1)
            parts.append(jnp.dot(lhs_g[...], right, preferred_element_type=f32))
        for j in range(nx):
            rows = [part[j * 2 * rl : (j + 1) * 2 * rl] for part in parts]
            spare = sz.mr - sz.pair * 2 * rl
            if spare:
                rows.append(jnp.zeros((spare, sz.cw), f32))
            sg[i, j] = jnp.concatenate(rows, axis=0).astype(bf16)

        def send(d):
            p = px(d + 1)
            remote(
                sg.at[i, p], rg.at[i, mx], g_ss.at[i, p], g_rs.at[i, mx], "gx", p
            ).start()

        each(nx - 1, send)
        rg[i, mx] = sg[i, mx]
        return carry

    lax.fori_loop(0, sz.msgs, gate_cols, 0)

    def t_recv(d):
        p = px(d + 1)
        return remote(ts_s.at[p], ts_r.at[p], t_ss.at[p], t_rs.at[p], "gx", p)

    each(nx - 1, lambda d: t_recv(d).wait_recv())
    scale_two = lax.rsqrt(add_up(ts_r, nx)[:, :1] / model_width + norm_eps)

    def hid_send(i, d):
        p = px(d + 1)
        cols = hid.at[i, mx]
        return remote(cols, cols, u_ss.at[i, p], u_rs.at[i, mx], "gx", p)

    def hid_recv(i, d):
        p = px(d + 1)
        cols = hid.at[i, p]
        return remote(cols, cols, u_ss.at[i, p], u_rs.at[i, p], "gx", p)

    def act_cols(i, carry):
        def arrive(d):
            p = px(d + 1)
            remote(
                sg.at[i, p], rg.at[i, p], g_ss.at[i, p], g_rs.at[i, p], "gx", p
            ).wait_recv()

        each(nx - 1, arrive)
        total = add_up(rg.at[i], nx)
        total = jnp.concatenate([total, jnp.zeros((rb, sz.cw), f32)], axis=0)
        for a in range(sz.pair):
            at = a * 2 * rl
            gate = total[at : at + rb] * scale_two
            up = total[at + rl : at + rl + rb] * scale_two
            value = gate / (1.0 + jnp.exp(-gate)) * up
            hid[i, mx, :, a * sz.cw : (a + 1) * sz.cw] = value.astype(bf16)
        each(nx - 1, lambda d: hid_send(i, d).start())
        return carry

    lax.fori_loop(0, sz.msgs, act_cols, 0)
    for i in range(sz.dcb):
        wd_copy(i).wait()

    def hid_wait(i, carry):
        each(nx - 1, lambda d: hid_recv(i, d).wait_recv())
        return carry

    lax.fori_loop(0, sz.msgs, hid_wait, 0)
    span = sz.pair * sz.cw
    for i in range(sz.dcb // 2):
        part = None
        for k in range(sz.msgs):
            right = jnp.concatenate(
                [wd_tile(2 * i + b)[k * span : (k + 1) * span] for b in range(2)], axis=1
            )
            d = jnp.dot(hid[k].reshape(rp, span), right, preferred_element_type=f32)
            part = d if part is None else part + d
        pa[:, :, i * step : (i + 1) * step] = part.astype(bf16).reshape(ny, sz.ra, step)
    out_ref[...] = mixed[...] + all_reduce(pa, dr, dall, c_ss, c_rs, d_ss, d_rs)

    each(nx - 1, lambda d: s_send(d).wait_send())
    each(nx - 1, lambda d: q_send(d).wait_send())
    each(nx - 1, lambda d: h_send(d).wait_send())
    each(nx - 1, lambda d: t_send(d).wait_send())

    def sent(i, carry):
        def one(d):
            p = px(d + 1)
            remote(
                sg.at[i, p], rg.at[i, mx], g_ss.at[i, p], g_rs.at[i, mx], "gx", p
            ).wait_send()
            hid_send(i, d).wait_send()

        each(nx - 1, one)
        return carry

    lax.fori_loop(0, sz.msgs, sent, 0)


def on_device(
    states,
    lengths,
    attn_gain,
    mlp_gain,
    w_qkv,
    b_qkv,
    key_cache,
    value_cache,
    w_out,
    w_gate_up,
    w_down,
):
    nx, ny = lax.axis_size("gx"), lax.axis_size("gy")
    rollouts, new, width = states.shape
    owned, slots, kv, head = key_cache.shape
    group = w_qkv.shape[2] // head - 2
    hidden = w_gate_up.shape[2]
    sz = Sizes(nx, ny, rollouts * new, width, kv, slots, hidden, group, new)
    x = jnp.pad(
        states.reshape(nx, sz.rl, width), ((0, 0), (0, sz.rb - sz.rl), (0, 0))
    ).reshape(sz.rp, width)
    bias = b_qkv.reshape(1, kv * sz.qw)
    inner = (kv,) if kv > 1 else ()
    kcache = key_cache.reshape((owned * slots,) + inner + (head,))
    vcache = value_cache.reshape((owned * slots,) + inner + (head,))
    wq = w_qkv.reshape((width,) + inner + (sz.qw,))
    wo = w_out.reshape(kv * group * head, width)
    dma = pltpu.SemaphoreType.DMA
    vm = pltpu.VMEM
    heads_w = kv * group * head
    newk = -(-kv * sz.rb // LANES) * LANES
    scratch = [
        vm((sz.qcb, width) + inner + (LANES,), bf16),
        vm((sz.dcb // 2, 2 * heads_w, LANES), bf16),
        vm((sz.hcb, width, 2, LANES), bf16),
        vm((max(1, sz.dcb - sz.second), hidden if sz.second < sz.dcb else 16, LANES), bf16),
        vm(kcache.shape, bf16),
        vm(vcache.shape, bf16),
        vm((max(kv * sz.rp, 2 * sz.rl * nx), 2 * width), bf16),
        vm((nx, sz.rb, kv * sz.qw), bf16),
        vm((nx, sz.rb, kv * sz.qw), bf16),
        vm((nx, sz.rb, LANES), f32),
        vm((nx, sz.rb, LANES), f32),
        vm((kv * group * sz.rb, LANES), bf16),
        vm((newk, LANES), bf16),
        vm((newk, LANES), bf16),
        vm((nx, sz.rb, heads_w), bf16),
        vm((ny, sz.ra, width), bf16),
        vm((ny, sz.ra, width), bf16),
        vm((ny, sz.ra, width), bf16),
        vm((sz.rp, width), f32),
        vm((nx, sz.rb, LANES), f32),
        vm((nx, sz.rb, LANES), f32),
        vm((sz.msgs, nx, sz.mr, sz.cw), bf16),
        vm((sz.msgs, nx, sz.mr, sz.cw), bf16),
        vm((sz.msgs, nx, sz.rb, sz.pair * sz.cw), bf16),
        vm((ny, sz.ra, width), bf16),
        vm((ny, sz.ra, width), bf16),
        dma((sz.qcb,)),
        dma((sz.dcb // 2, 2)),
        dma((sz.hcb,)),
        dma((sz.dcb,)),
        dma((2,)),
    ]
    scratch += [dma((nx,))] * 6 + [dma((ny,))] * 4 + [dma((nx,))] * 2
    scratch += [dma((sz.msgs, nx))] * 4 + [dma((ny,))] * 4
    anyspec = pl.BlockSpec(memory_space=pl.ANY)
    vspec = pl.BlockSpec(memory_space=pltpu.VMEM)
    out = pl.pallas_call(
        functools.partial(kernel, sz, width * nx),
        out_shape=jax.ShapeDtypeStruct((sz.rp, width), f32),
        in_specs=[pl.BlockSpec(memory_space=pltpu.SMEM)] + [vspec] * 4 + [anyspec] * 6,
        out_specs=vspec,
        scratch_shapes=scratch,
        compiler_params=pltpu.CompilerParams(
            collective_id=0, has_side_effects=True, vmem_limit_bytes=63 * 2**20
        ),
    )(
        lengths,
        x,
        attn_gain.reshape(1, width),
        mlp_gain.reshape(1, width),
        bias,
        wq,
        kcache,
        vcache,
        wo,
        w_gate_up,
        w_down,
    )
    out = out.reshape(nx, sz.rb, width)[:, : sz.rl]
    return out.reshape(rollouts, new, width)


def solution(mesh):
    in_specs = (
        P("groups", None, "gx"),
        P(("groups", "gx")),
        P("gx"),
        P("gx"),
        P("gx", "gy", None),
        P("gy", None),
        P(("groups", "gx"), None, "gy", None),
        P(("groups", "gx"), None, "gy", None),
        P("gy", None, "gx"),
        P("gx", None, "gy"),
        P("gy", "gx"),
    )
    out_specs = P("groups", None, "gx")
    return jax.shard_map(
        on_device, mesh=mesh, in_specs=in_specs, out_specs=out_specs, check_vma=False
    )
```

time: 233 us -> 92.9 us (0.40); the launches traced: 230 us -> 92.7 us
  Pallas kernels: 0 us -> 87.6 us
  blocking collectives: 73.5 us -> 0 us
  waiting for transfers between devices: 60.9 us -> 0 us
  matrix products: 37.3 us -> 0 us
  local copies, waits for them, and re-layouts: 35.7 us -> 5.04 us
  between operations: 14.4 us -> 0.01 us
  other arithmetic: 5.61 us -> 0 us
  starting transfers between devices: 2.88 us -> 0 us
    pallas_call x0 -> x1, Pallas kernels: none -> 87.6 us  [on_device(): pl.pallas_call(functools.partial(kernel, sz, width * nx), out_shape=jax.S...]
    psum x2 -> x0, waiting for transfers between devices: 57.3 us -> none  [the longest x1 39.5 us: on_device(): lax.psum(down_part.astype(jnp.bfloat16), 'gy').astype(jnp.float32)]
    dot_general x8 -> x0, matrix products: 37.3 us -> none  [the longest x1 15.7 us: on_device(): jnp.dot(normed_two, flat_gate_up, preferred_element_type=jnp.float32)]
    unnamed x28 -> x1, local copies, waits for them, and re-layouts: 33.8 us -> 1.29 us
    unnamed x2 -> x0, blocking collectives: 28.8 us -> none
    all_gather x2 -> x0, blocking collectives: 23.7 us -> none  [the longest x1 12.8 us: on_device(): lax.all_gather(hidden_share, 'gx', axis=0, tiled=True)]
    psum x2 -> x0, blocking collectives: 21 us -> none  [the longest x1 10.8 us: on_device(): squares = lax.psum(jnp.sum(resid * resid, axis=1), 'gx')]
    unnamed x4 -> x0, waiting for transfers between devices: 3.67 us -> none
  transfers between devices with their start and end apart: 4 -> 0, of which waited for: 3 -> 0; matrix products, arithmetic and copies ran while one was open for 10% -> 0% of each run, Pallas kernels for 0% -> 0%
where the time goes in v1:
time: 92.9 us; the launch traced here: 92.7 us
  Pallas kernels  87.6 us (94%)
  local copies, waits for them, and re-layouts  5.04 us (5%)
    pallas_call x1, Pallas kernels, on_device(): pl.pallas_call(functools.partial(kernel, sz, width * nx), out_shape=jax.S...  87.6 us
    reshape x1, local copies, waits for them, and re-layouts, on_device(): return out.reshape(rollouts, new, width)  2.01 us

profile of v1, /device:TPU:1, one launch (start us, length us, event | category | flops | bytes accessed | tf_op | source)
XLA Modules:
  0.0 92.7 jit_solution(13916580791276562008)
XLA Ops:
  0.0 1.3 %copy.12 = bf16[1,1,2,1280]{3,1,2,0:T(2,128)(2,1)} copy(bf16[1,1,2,1280]{3,2,1,0:T(2,128)(2,1)} %bitcast.19) | data formatting | bytes 10240
  1.3 1.0 %reshape.30 = bf16[4,12,2048]{2,1,0:T(8,128)(2,1)S(1)} reshape(bf16[24,2,2048]{2,1,0:T(2,128)(2,1)} %param.11) | data formatting | bytes 393216 | tf_op jit(solution)/shard_map/reshape | solution.py:549
  2.3 0.7 pad.4
  3.0 87.6 %shard_map.109 = f32[64,2048]{1,0:T(8,128)} custom-call(s32[6]{0:T(128)} %lens.1, bf16[64,2048]{1,0:T(8,128)(2,1)} %bitcast.13, f32[1,2048]{1,0:T(1,128)} %bitcast.17, f32[1,2048]{1,0:T(1,128)} %bitcast.18, bf16[1,2560]{1,0:T(2,128)(2,1)} %bitcast.16, bf16[2048,2,1280]{2,1,0:T(2,128)(2,1)} %wq_hbm.1, bf16[768,2,128]{2,1,0:T(2,128)(2,1)} %bitcast.14, ...), custom_call_target="tpu_custom_call" | custom-call | tf_op jit(solution)/shard_map/pallas_call | solution.py:598
  90.7 2.0 %reshape.39 = f32[24,2,2048]{2,1,0:T(2,128)} reshape(f32[4,12,2048]{2,1,0:T(8,128)} %bitcast.12) | data formatting | bytes 786432 | tf_op jit(solution)/shard_map/reshape | solution.py:621

commit v2 on v1

--- a/solution.py
+++ b/solution.py
@@ -244,21 +244,32 @@
         right = jnp.concatenate([wq_tile(2 * i)[...], wq_tile(2 * i + 1)[...]], axis=1)
         part = jnp.dot(lhs_q[...], right, preferred_element_type=f32).astype(bf16)
         for h in range(kv):
-            at = pl.multiple_of(h * sz.qw + i * 2 * LANES, 2 * LANES)
-            sq[:, :, pl.ds(at, 2 * LANES)] = part[h * rp : (h + 1) * rp].reshape(nx, rb, 2 * LANES)
+            sq[i, :, :, h * 2 * LANES : (h + 1) * 2 * LANES] = part[
+                h * rp : (h + 1) * rp
+            ].reshape(nx, rb, 2 * LANES)
+        each(nx - 1, lambda d: q_send(i, d).start())
+        rq[i, mx] = sq[i, mx]
         return carry
 
+    def q_send(i, d):
+        p = px(d + 1)
+        return remote(sq.at[i, p], rq.at[i, mx], q_ss.at[i, p], q_rs.at[i, mx], "gx", p)
+
+    def q_recv(i, d):
+        p = px(d + 1)
+        return remote(sq.at[i, p], rq.at[i, p], q_ss.at[i, p], q_rs.at[i, p], "gx", p)
+
+    def over_chunks(body):
+        def step(i, carry):
+            each(nx - 1, lambda d: body(i, d))
+            return carry
+
+        lax.fori_loop(0, sz.qcb // 2, step, 0)
+
     lax.fori_loop(0, sz.qcb // 2, qkv_cols, 0)
 
-    def q_send(d):
-        p = px(d + 1)
-        return remote(sq.at[p], rq.at[mx], q_ss.at[p], q_rs.at[mx], "gx", p)
-
-    each(nx - 1, lambda d: q_send(d).start())
     for i in range(sz.reuse):
         wd_copy(i).start()
-
-    rq[mx] = sq[mx]
 
     def gathered(buf_s, buf_r, ss, rs, d):
         p = px(d + 1)
@@ -276,7 +287,7 @@
     sine = jnp.where(iota((rb, LANES), 1) < half, -jnp.sin(angle), jnp.sin(angle))
 
     each(nx - 1, lambda d: gathered(ss_s, ss_r, s_ss, s_rs, d).wait_recv())
-    each(nx - 1, lambda d: gathered(sq, rq, q_ss, q_rs, d).wait_recv())
+    over_chunks(lambda i, d: q_recv(i, d).wait_recv())
 
     def add_up(buf, n):
         if n <= 4:
@@ -289,7 +300,9 @@
         )
 
     scale = lax.rsqrt(add_up(ss_r, nx)[:, :1] / model_width + norm_eps)
-    qkv = add_up(rq, nx) * scale + bq_ref[...].astype(f32)
+    sums = [add_up(rq.at[i], nx) for i in range(sz.qcb // 2)]
+    sums = [t[:, h * 2 * LANES : (h + 1) * 2 * LANES] for h in range(kv) for t in sums]
+    qkv = jnp.concatenate(sums, axis=1) * scale + bq_ref[...].astype(f32)
 
     def rotate(v):
         return (v * cosine + pltpu.roll(v, half, 1) * sine).astype(bf16)
@@ -427,10 +440,13 @@
         for a in range(sz.pair):
             for c in range(sz.cb):
                 wg_copy((i * sz.pair + a) * sz.cb + c).wait()
+        first = i * sz.pair * sz.cb
+        right = jnp.concatenate(
+            [wg_tile(first + c)[...] for c in range(sz.pair * sz.cb)], axis=1
+        )
+        both = jnp.dot(lhs_g[...], right, preferred_element_type=f32)
         for a in range(sz.pair):
-            first = (i * sz.pair + a) * sz.cb
-            right = jnp.concatenate([wg_tile(first + c)[...] for c in range(sz.cb)], axis=1)
-            parts.append(jnp.dot(lhs_g[...], right, preferred_element_type=f32))
+            parts.append(both[:, a * sz.cw : (a + 1) * sz.cw])
         for j in range(nx):
             rows = [part[j * 2 * rl : (j + 1) * 2 * rl] for part in parts]
             spare = sz.mr - sz.pair * 2 * rl
@@ -508,7 +524,7 @@
     out_ref[...] = mixed[...] + all_reduce(pa, dr, dall, c_ss, c_rs, d_ss, d_rs)
 
     each(nx - 1, lambda d: s_send(d).wait_send())
-    each(nx - 1, lambda d: q_send(d).wait_send())
+    over_chunks(lambda i, d: q_send(i, d).wait_send())
     each(nx - 1, lambda d: h_send(d).wait_send())
     each(nx - 1, lambda d: t_send(d).wait_send())
 
@@ -566,8 +582,8 @@
         vm(kcache.shape, bf16),
         vm(vcache.shape, bf16),
         vm((max(kv * sz.rp, 2 * sz.rl * nx), 2 * width), bf16),
-        vm((nx, sz.rb, kv * sz.qw), bf16),
-        vm((nx, sz.rb, kv * sz.qw), bf16),
+        vm((sz.qcb // 2, nx, sz.rb, kv * 2 * LANES), bf16),
+        vm((sz.qcb // 2, nx, sz.rb, kv * 2 * LANES), bf16),
         vm((nx, sz.rb, LANES), f32),
         vm((nx, sz.rb, LANES), f32),
         vm((kv * group * sz.rb, LANES), bf16),
@@ -591,7 +607,7 @@
         dma((sz.dcb,)),
         dma((2,)),
     ]
-    scratch += [dma((nx,))] * 6 + [dma((ny,))] * 4 + [dma((nx,))] * 2
+    scratch += [dma((sz.qcb // 2, nx))] * 2 + [dma((nx,))] * 4 + [dma((ny,))] * 4 + [dma((nx,))] * 2
     scratch += [dma((sz.msgs, nx))] * 4 + [dma((ny,))] * 4
     anyspec = pl.BlockSpec(memory_space=pl.ANY)
     vspec = pl.BlockSpec(memory_space=pltpu.VMEM)

time: 92.9 us -> 89.7 us (0.966)
  Pallas kernels: 87.6 us -> 84.4 us
    pallas_call x1, Pallas kernels: 87.6 us -> 84.4 us  [on_device(): pl.pallas_call(functools.partial(kernel, sz, width * nx), out_shape=jax.S...]
where the time goes in v2:
time: 89.7 us; the launch traced here: 89.4 us
  Pallas kernels  84.4 us (94%)
  local copies, waits for them, and re-layouts  5.04 us (6%)
    pallas_call x1, Pallas kernels, on_device(): pl.pallas_call(functools.partial(kernel, sz, width * nx), out_shape=jax.S...  84.4 us
    reshape x1, local copies, waits for them, and re-layouts, on_device(): return out.reshape(rollouts, new, width)  2.01 us

profile of v2, /device:TPU:1, one launch (start us, length us, event | category | flops | bytes accessed | tf_op | source)
XLA Modules:
  0.0 89.4 jit_solution(14852773062919468936)
XLA Ops:
  0.0 1.3 %copy.12 = bf16[1,1,2,1280]{3,1,2,0:T(2,128)(2,1)} copy(bf16[1,1,2,1280]{3,2,1,0:T(2,128)(2,1)} %bitcast.19) | data formatting | bytes 10240
  1.3 1.0 %reshape.30 = bf16[4,12,2048]{2,1,0:T(8,128)(2,1)S(1)} reshape(bf16[24,2,2048]{2,1,0:T(2,128)(2,1)} %param.11) | data formatting | bytes 393216 | tf_op jit(solution)/shard_map/reshape | solution.py:565
  2.3 0.7 pad.4
  3.0 84.4 %shard_map.109 = f32[64,2048]{1,0:T(8,128)} custom-call(s32[6]{0:T(128)} %lens.1, bf16[64,2048]{1,0:T(8,128)(2,1)} %bitcast.13, f32[1,2048]{1,0:T(1,128)} %bitcast.17, f32[1,2048]{1,0:T(1,128)} %bitcast.18, bf16[1,2560]{1,0:T(2,128)(2,1)} %bitcast.16, bf16[2048,2,1280]{2,1,0:T(2,128)(2,1)} %wq_hbm.1, bf16[768,2,128]{2,1,0:T(2,128)(2,1)} %bitcast.14, ...), custom_call_target="tpu_custom_call" | custom-call | tf_op jit(solution)/shard_map/pallas_call | solution.py:614
  87.4 2.0 %reshape.39 = f32[24,2,2048]{2,1,0:T(2,128)} reshape(f32[4,12,2048]{2,1,0:T(8,128)} %bitcast.12) | data formatting | bytes 786432 | tf_op jit(solution)/shard_map/reshape | solution.py:637
